TPU v7x, 32 devices: a whole 2x2x4 slice. The times are simulated.
32 devices in a mesh: half: 2 (over y), rows: 16 (over z, x, core).
Axes of the slice: x: 2, y: 2, z: 4, core: 2. Of those that a mesh axis runs over, the one named last changes fastest.
Arguments:
- frames: bfloat16 [16384, 3000], P(('half', 'rows')), may hold values from -8 to 8
- labels: int32 [16384], P(('half', 'rows')), may hold values from 0 to 1, as said below
- counts: int32 [32], P(('half', 'rows')), may hold values from 256 to 512, as said below
- seeds: int32 [2, 512], P('half', 'rows'), may hold values from 0 to 511
Outputs:
- means: float32 [2, 512, 3000], P('half', 'rows')
- occupancy: float32 [2, 512], P('half', 'rows')
Inputs may be any that keep to these rules, and one draw needn't show every extreme that they name: `labels`: on each device of half h, live frames carry child h except for at most 256 of them, which carry 1 - h; exactly 256 do on some device. Frames that are not live carry h. `counts`: 512 on some device.
All inputs are finite; a program needn't handle non-finite values.
Results may differ from a plain program's by a relative error of at most 0.0014.
Values may be sent and summed in bfloat16 or wider, within the bound.
A program may use at most 128 MiB of HBM per device.

v0:
```python
import functools
import math

import jax
import jax.numpy as jnp
from jax import lax
from jax.experimental import pallas as pl
from jax.experimental.pallas import tpu as pltpu
from jax.sharding import PartitionSpec as P


def from_partner(value, axis, stride):
    mask = 2**stride
    pairs = [(source, source ^ mask) for source in range(lax.axis_size(axis))]
    return lax.ppermute(value, axis, pairs)


def score_piece(rows_in, piece):
    cross = lax.dot_general(
        rows_in, piece, (((1,), (1,)), ((), ())), preferred_element_type=jnp.float32
    )
    wide = piece.astype(jnp.float32)
    return (cross - 0.5 * jnp.sum(wide * wide, axis=1)[None, :]) / math.sqrt(rows_in.shape[1])


def soft_weights(logits, valid):
    top = jnp.max(logits, axis=1, keepdims=True)
    expo = jnp.exp(logits - top)
    total = jnp.sum(expo, axis=1, keepdims=True)
    return (expo / total * valid[:, None]).astype(jnp.bfloat16)


def weighted(weights, rows_in):
    return lax.dot_general(
        weights, rows_in, (((0,), (0,)), ((), ())), preferred_element_type=jnp.float32
    )


def column_mass(weights):
    return jnp.sum(weights.astype(jnp.float32), axis=0)


def shards(frames, labels, counts, seeds):
    rows_dev = frames.shape[0]
    cap = rows_dev // 2
    side = lax.axis_index("half")
    spots = jnp.arange(rows_dev, dtype=jnp.int32)
    live = spots < counts[0]
    foreign = live & (labels != side)
    native = (live & (labels == side)).astype(jnp.float32)
    order = jnp.argsort(jnp.where(foreign, 0, 1).astype(jnp.int32), stable=True)
    picked = order[:cap]
    moved = frames[picked]
    flag = foreign[picked].astype(jnp.float32)
    mine = frames[seeds[0]]
    got_rows, got_flag = from_partner((moved, flag.astype(jnp.bfloat16)), "half", 0)
    pool = jnp.concatenate([frames, got_rows], axis=0)
    valid = jnp.concatenate([native, got_flag.astype(jnp.float32)])
    logits = score_piece(pool, lax.all_gather(mine, "rows", axis=0, tiled=True))
    weights = soft_weights(logits, valid)
    sums, mass = (
        lax.psum_scatter(weighted(weights, pool), "rows", scatter_dimension=0, tiled=True),
        lax.psum_scatter(column_mass(weights), "rows", scatter_dimension=0, tiled=True),
    )
    whole_k = mass.shape[0] * lax.axis_size("rows")
    total_slots = rows_dev * lax.axis_size("half") * lax.axis_size("rows")
    means = sums / (mass + 1.0)[:, None]
    occupancy = mass * (2.0 * whole_k / total_slots)
    return (means[None], occupancy[None])


MESH = pl.DeviceIdType.MESH
WIRE = jnp.bfloat16
STEP = 512
PART = 128
LAG = 3
NT = (((1,), (1,)), ((), ()))
NN = (((1,), (0,)), ((), ()))


def round_up(value, unit):
    return -(-value // unit) * unit


def dot(a, b, how):
    return lax.dot_general(a, b, how, preferred_element_type=jnp.float32)


def column_weights(cross, norm, width, valid):
    logits = (cross - 0.5 * norm) / math.sqrt(width)
    top = jnp.max(logits, axis=0, keepdims=True)
    expo = jnp.exp(logits - top)
    total = jnp.sum(expo, axis=0, keepdims=True)
    return (expo / total * valid).astype(jnp.bfloat16)


def level(
    outer, width,
    x_ref, tail_ref, labels_ref, counts_ref, seeds_ref,
    out_ref,
    xf, table, gone, came, squares, cross, near, weights,
    keep, csend, crecv, keepx, xsend, xrecv, zsend, zrecv,
    x_load, y_out, y_in, u_out, d_out, t_out, t_in, c_out, c_in, x_out, x_in, z_out, z_in,
):
    slots = xf.shape[2]
    shard = seeds_ref.shape[1]
    steps = xf.shape[0]
    parts = gone.shape[0]
    sent = y_rows(width)
    whole = steps - 1
    rest = width - whole * STEP
    half_k = keep.shape[1]
    quarter_k = keepx.shape[1]
    side = lax.axis_index("half")
    row = lax.axis_index("rows")
    twin = row + 1 - 2 * (row % 2)
    across = row + 2 - 4 * ((row // 2) % 2)
    along = [
        ((row // 4 + d) % outer) * 4 + row % 4 for d in range(1, outer)
    ]

    barrier = pltpu.get_barrier_semaphore()
    pl.semaphore_signal(barrier, inc=1, device_id=(1 - side, row), device_id_type=MESH)
    for peer in [twin, across] + along:
        pl.semaphore_signal(barrier, inc=1, device_id=(side, peer), device_id_type=MESH)

    def load(c):
        at = pl.ds(pl.multiple_of(c * STEP, STEP), STEP)
        return pltpu.make_async_copy(x_ref.at[at], xf.at[c], x_load.at[c])

    @pl.loop(0, whole)
    def _(c):
        load(c).start()

    def remote(src, dst, out_sem, in_sem, where):
        return pltpu.make_async_remote_copy(
            src_ref=src, dst_ref=dst, send_sem=out_sem, recv_sem=in_sem,
            device_id=where, device_id_type=MESH,
        )

    labels = labels_ref[...]
    spots = lax.broadcasted_iota(jnp.int32, (1, slots), 1)
    live = spots < counts_ref[0]
    native = (live & (labels == side)).astype(jnp.float32)
    foreign = jnp.where(live & (labels != side), 1.0, 0.0)
    upper = (
        lax.broadcasted_iota(jnp.int32, (slots, slots), 0)
        <= lax.broadcasted_iota(jnp.int32, (slots, slots), 1)
    ).astype(jnp.float32).astype(jnp.bfloat16)
    rank = dot(jnp.broadcast_to(foreign, (16, slots)).astype(jnp.bfloat16), upper, NN)[:1]
    place = jnp.where(foreign > 0, rank - 1.0, -1.0).astype(jnp.int32)

    xf[whole, pl.ds(0, rest), :] = tail_ref[pl.ds(0, rest), :]
    fill = lax.broadcasted_iota(jnp.int32, (STEP - rest, slots), 0) == 0
    xf[whole, pl.ds(rest, STEP - rest), :] = fill.astype(jnp.float32).astype(jnp.bfloat16)

    def pick(part):
        lane = lax.broadcasted_iota(jnp.int32, (PART, slots), 0) + part * PART
        return (lane == place).astype(jnp.float32).astype(jnp.bfloat16)

    def y_copy(part, c, rows=STEP):
        at = pl.ds(c * STEP, rows)
        return remote(
            gone.at[part, at], came.at[part, at],
            y_out.at[part, c], y_in.at[part, c], (1 - side, row),
        )

    last_rows = sent - whole * STEP

    def each_y(part, act):
        @pl.loop(0, whole)
        def _(c):
            act(y_copy(part, c))

        act(y_copy(part, whole, last_rows))

    first = pick(0)
    pl.semaphore_wait(barrier, outer + 2)

    @pl.loop(0, whole)
    def _(c):
        at = pl.ds(pl.multiple_of(c * STEP, STEP), STEP)
        load(c).wait()
        gone[0, at, :] = dot(xf[c], first, NT).astype(jnp.bfloat16)
        y_copy(0, c).start()

    gone[0, pl.ds(whole * STEP, STEP), :] = dot(xf[whole], first, NT).astype(jnp.bfloat16)
    y_copy(0, whole, last_rows).start()

    seeds = jnp.broadcast_to(seeds_ref[...], (shard, shard))
    diagonal = lax.broadcasted_iota(jnp.int32, (shard, shard), 0) == lax.broadcasted_iota(
        jnp.int32, (shard, shard), 1
    )
    seed = jnp.sum(jnp.where(diagonal, seeds, 0), axis=1, keepdims=True)
    chosen = (
        lax.broadcasted_iota(jnp.int32, (shard, slots), 1) == seed
    ).astype(jnp.float32).astype(jnp.bfloat16)

    @pl.loop(0, steps)
    def _(c):
        at = pl.ds(pl.multiple_of(c * STEP, STEP), STEP)
        lane = lax.broadcasted_iota(jnp.int32, (shard, STEP), 1) + c * STEP
        mine = dot(chosen, xf[c], NT)
        table[pl.ds(0, shard), at] = jnp.where(lane < width, mine, 0.0).astype(jnp.bfloat16)

    def t_copy(index, source, target, where):
        return remote(
            table.at[pl.ds(source * shard, shard)], table.at[pl.ds(target * shard, shard)],
            t_out.at[index], t_in.at[target], (side, where),
        )

    def up_copy(k):
        where = lax.rem(row + 4, outer * 4)
        return remote(
            table.at[pl.ds((outer - k) % outer * shard, shard)],
            table.at[pl.ds((outer - k - 1) * shard, shard)],
            u_out.at[k], t_in.at[outer - k - 1], (side, where),
        )

    def down_copy(k):
        where = lax.rem(row + (outer - 1) * 4, outer * 4)
        return remote(
            table.at[pl.ds(k * shard, shard)], table.at[pl.ds((k + 1) * shard, shard)],
            d_out.at[k], t_in.at[k + 1], (side, where),
        )

    x_gather = [t_copy(s, s, outer + s, across) for s in range(outer)]
    c_gather = [t_copy(outer + s, s, 2 * outer + s, twin) for s in range(2 * outer)]
    depth = row // 4

    @pl.when(depth > 0)
    def _():
        down_copy(0).start()

    @pl.when(depth < outer - 1)
    def _():
        up_copy(0).start()

    x_gather[0].start()
    c_gather[0].start()

    for part in range(1, parts):
        later = pick(part)

        @pl.loop(0, steps)
        def _(c):
            at = pl.ds(pl.multiple_of(c * STEP, STEP), STEP)
            gone[part, at, :] = dot(xf[c], later, NT).astype(jnp.bfloat16)

        each_y(part, lambda copy: copy.start())
    if steps * STEP > sent:
        for part in range(parts):
            came[part, pl.ds(sent, steps * STEP - sent), :] = jnp.zeros(
                (steps * STEP - sent, PART), jnp.bfloat16
            )

    def arrived(slot):
        return t_copy(0, 0, slot, twin).wait_recv()

    def from_above(k):
        arrived(k)

        @pl.when(depth > 0)
        def _():
            down_copy(k).start()

        x_gather[k].start()
        c_gather[k].start()

    def from_below(k):
        arrived(outer - k)

        @pl.when(depth < outer - 1)
        def _():
            up_copy(k).start()

        x_gather[outer - k].start()
        c_gather[outer - k].start()

    def crossed(s):
        x_gather[s].wait_recv()
        c_gather[outer + s].start()

    def both(k, above, below):
        @pl.when(depth + k <= outer - 1)
        def _():
            above(k)

        @pl.when(depth >= k)
        def _():
            below(k)

    for k in range(1, outer):
        both(k, from_above, from_below)
        if k == 1:
            crossed(0)
        else:
            both(k - 1, crossed, lambda back: crossed(outer - back))
    squares[...] = jnp.zeros_like(squares)
    near[...] = jnp.zeros_like(near)

    def score(group):
        rows_at = pl.ds(group * quarter_k, quarter_k)

        @pl.loop(0, steps)
        def _(c):
            at = pl.ds(pl.multiple_of(c * STEP, STEP), STEP)
            block = table[rows_at, at]
            near[rows_at, :] += dot(block, xf[c], NN)
            wide = block.astype(jnp.float32)
            wide = wide * wide
            total = wide[:, :PART]
            for lane in range(PART, STEP, PART):
                total += wide[:, lane : lane + PART]
            squares[rows_at, :] += total

    score(0)
    for s in range(outer):
        c_gather[s].wait_recv()
    score(2)
    both(outer - 1, crossed, lambda back: crossed(outer - back))
    score(1)
    for s in range(outer, 2 * outer):
        c_gather[s].wait_recv()
    score(3)

    norm = jnp.sum(squares[...], axis=1, keepdims=True)
    weights[:, pl.ds(0, slots)] = column_weights(near[...], norm, width, native)

    for part in range(parts):
        cross[...] = jnp.zeros_like(cross)

        @pl.loop(0, steps)
        def _(c):
            @pl.when(c < whole)
            def _():
                y_copy(part, c).wait_recv()

            @pl.when(c == whole)
            def _():
                y_copy(part, whole, last_rows).wait_recv()

            at = pl.ds(pl.multiple_of(c * STEP, STEP), STEP)
            cross[...] += dot(table[:, at], came[part, at, :], NN)

        flag = came[part, pl.ds(width // 16 * 16, 16), :].astype(jnp.float32)
        flag = flag[width % 16 : width % 16 + 1]
        weights[:, pl.ds(slots + part * PART, PART)] = column_weights(
            cross[...], norm, width, flag
        )

    def narrow(c, ref, sums):
        ref[...] = sums.astype(WIRE)

        @pl.when(c == whole)
        def _():
            low = rest // PART * PART
            tile = sums[:, low : low + PART]
            lost = pltpu.roll(tile - tile.astype(WIRE).astype(jnp.float32), 1, 1)
            lane = lax.broadcasted_iota(jnp.int32, tile.shape, 1)
            tile = jnp.where(lane == rest - low + 1, tile + lost, tile)
            ref[:, low : low + PART] = tile.astype(WIRE)

    def c_copy(c):
        return remote(csend.at[c], crecv.at[c], c_out.at[c], c_in.at[c], (side, twin))

    def x_copy(c):
        return remote(xsend.at[c], xrecv.at[c], x_out.at[c], x_in.at[c], (side, across))

    def z_copy(c, d):
        return remote(
            zsend.at[c, d - 1], zrecv.at[c, d - 1],
            z_out.at[c, d - 1], z_in.at[c, d - 1], (side, along[d - 1]),
        )

    def add_up(c):
        at = pl.ds(pl.multiple_of(c * STEP, STEP), STEP)
        block = jnp.concatenate(
            [xf[c]] + [came[part, at, :] for part in range(parts)], axis=1
        )
        sums = dot(weights[...], block, NT)
        csend[c] = sums[half_k:]
        c_copy(c).start()
        keep[c] = sums[:half_k]

    def to_across(c):
        c_copy(c).wait_recv()
        sums = keep[c] + crecv[c]
        narrow(c, xsend.at[c], sums[quarter_k:])
        x_copy(c).start()
        keepx[c] = sums[:quarter_k]

    def to_along(c):
        x_copy(c).wait_recv()
        sums = keepx[c] + xrecv[c].astype(jnp.float32)
        for d in range(1, outer):
            narrow(c, zsend.at[c, d - 1], sums[d * shard : (d + 1) * shard])
        for d in range(1, outer):
            z_copy(c, d).start()
        keepx[c, pl.ds(0, shard), :] = sums[:shard]

    @pl.loop(0, steps + LAG)
    def _(c):
        @pl.when(c < steps)
        def _():
            add_up(c)

        @pl.when((c > 0) & (c <= steps))
        def _():
            to_across(c - 1)

        @pl.when(c >= LAG)
        def _():
            to_along(c - LAG)

    @pl.loop(0, steps)
    def _(c):
        sums = keepx[c, pl.ds(0, shard), :]
        for d in range(1, outer):
            z_copy(c, d).wait_recv()
            sums += zrecv[c, d - 1].astype(jnp.float32)
        out_ref[:, pl.ds(pl.multiple_of(c * STEP, STEP), STEP)] = sums

    for copy in x_gather + c_gather:
        copy.wait_send()
    for k in range(outer - 1):
        @pl.when((depth > 0) & (depth + k <= outer - 1))
        def _():
            down_copy(k).wait_send()

        @pl.when((depth < outer - 1) & (depth >= k))
        def _():
            up_copy(k).wait_send()

    for part in range(parts):
        each_y(part, lambda copy: copy.wait_send())

    @pl.loop(0, steps)
    def _(c):
        c_copy(c).wait_send()
        x_copy(c).wait_send()
        for d in range(1, outer):
            z_copy(c, d).wait_send()


def y_rows(width):
    return round_up(width + 1, 16)


def fused(frames, labels, counts, seeds):
    slots, width = frames.shape
    shard = seeds.shape[1]
    n_rows = lax.axis_size("rows")
    outer = n_rows // 4
    whole_k = shard * n_rows
    parts = slots // 2 // PART
    padded = round_up(width + 1, STEP)
    steps = padded // STEP
    dma = pltpu.SemaphoreType.DMA
    bf16, f32 = jnp.bfloat16, jnp.float32
    flops = 4 * (slots + slots // 2) * whole_k * width
    vmem = pl.BlockSpec(memory_space=pltpu.VMEM)
    sums = pl.pallas_call(
        functools.partial(level, outer, width),
        out_shape=jax.ShapeDtypeStruct((shard, padded), f32),
        grid=(1,),
        in_specs=[
            pl.BlockSpec(memory_space=pltpu.HBM),
            pl.BlockSpec((STEP, slots), lambda i: (steps - 1, 0)),
            vmem, pl.BlockSpec(memory_space=pltpu.SMEM),
            vmem,
        ],
        out_specs=vmem,
        scratch_shapes=[
            pltpu.VMEM((steps, STEP, slots), bf16),
            pltpu.VMEM((whole_k, padded), bf16),
            pltpu.VMEM((parts, padded, PART), bf16),
            pltpu.VMEM((parts, padded, PART), bf16),
            pltpu.VMEM((whole_k, PART), f32),
            pltpu.VMEM((whole_k, PART), f32),
            pltpu.VMEM((whole_k, slots), f32),
            pltpu.VMEM((whole_k, slots + parts * PART), bf16),
            pltpu.VMEM((steps, whole_k // 2, STEP), f32),
            pltpu.VMEM((steps, whole_k // 2, STEP), f32),
            pltpu.VMEM((steps, whole_k // 2, STEP), f32),
            pltpu.VMEM((steps, whole_k // 4, STEP), f32),
            pltpu.VMEM((steps, whole_k // 4, STEP), WIRE),
            pltpu.VMEM((steps, whole_k // 4, STEP), WIRE),
            pltpu.VMEM((steps, outer - 1, shard, STEP), WIRE),
            pltpu.VMEM((steps, outer - 1, shard, STEP), WIRE),
            dma((steps,)), dma((parts, steps)), dma((parts, steps)),
            dma((outer,)), dma((outer,)),
            dma((4 * outer,)), dma((4 * outer,)),
            dma((steps,)), dma((steps,)),
            dma((steps,)), dma((steps,)),
            dma((steps, outer - 1)), dma((steps, outer - 1)),
        ],
        compiler_params=pltpu.CompilerParams(
            collective_id=0, has_side_effects=True, vmem_limit_bytes=52 * 2**20
        ),
        cost_estimate=pl.CostEstimate(
            flops=flops, bytes_accessed=slots * width * 2, transcendentals=slots * whole_k
        ),
    )(frames.T, frames.T, labels[None], counts, seeds)
    mass = sums[:, width] + sums[:, width + 1]
    total_slots = slots * lax.axis_size("half") * n_rows
    means = sums[:, :width] / (mass + 1.0)[:, None]
    return (means[None], (mass * (2.0 * whole_k / total_slots))[None])


def fits(mesh, frames, seeds):
    sizes = dict(mesh.shape)
    n_half, n_rows = sizes["half"], sizes["rows"]
    slots = frames.shape[0] // (n_half * n_rows)
    shard = seeds.shape[1] // n_rows
    lone = frames.shape[1] % STEP > 0 and frames.shape[1] % PART < PART - 1
    return (
        n_half == 2 and n_rows % 4 == 0 and n_rows >= 8 and shard % 16 == 0 and shard > 0
        and slots % (2 * PART) == 0 and slots * n_half * n_rows == frames.shape[0]
        and slots <= 1024 and seeds.shape[1] <= 512 and frames.shape[1] <= 4096
        and frames.shape[1] > STEP and lone
    )


def solution(mesh):
    placed = (
        P(("half", "rows"), None),
        P(("half", "rows")),
        P(("half", "rows")),
        P("half", "rows"),
    )

    def run(frames, labels, counts, seeds):
        body = fused if fits(mesh, frames, seeds) else shards
        return jax.shard_map(
            body,
            mesh=mesh,
            in_specs=placed,
            out_specs=(P("half", "rows", None), P("half", "rows")),
            check_vma=False,
        )(frames, labels, counts, seeds)

    return run
```

profile of v0, /device:TPU:0, one launch (start us, length us, event | category | flops | bytes accessed | tf_op | source)
XLA Modules:
  0.0 72.4 jit_solution(2274802293580199192)
XLA Ops:
  1.3 0.0 copy-start
  1.3 0.7 copy-done
  2.0 0.0 copy-start.1
  2.0 0.7 copy-done.1
  2.6 68.2 %shard_map.59 = f32[32,3072]{1,0:T(8,128)S(1)} custom-call(bf16[3000,512]{1,0:T(8,128)(2,1)} %bitcast.7, bf16[3000,512]{1,0:T(8,128)(2,1)} %bitcast.8, s32[1,512]{1,0:T(1,128)S(1)} %bitcast.5, s32[1]{0:T(128)S(6)} %copy.6.counts_ref, s32[1,32]{1,0:T(1,128)S(1)} %copy-done.1), custom_call_target="tpu_custom_call" | custom-call | flops 4718592000 | bytes 3072000 | tf_op jit(solution)/shard_map/pallas_call | solution.py:463
  70.8 0.7 multiply_reduce_fusion
  71.5 0.8 %divide_bitcast_fusion = f32[1,32,3000]{2,1,0:T(8,128)} fusion(f32[32,3072]{1,0:T(8,128)S(1)} %shard_map.59, f32[32]{0:T(128)S(1)} %get-tuple-element.3), kind=kLoop, calls=%fused_computation | loop fusion | flops 96000 | bytes 768128 | tf_op jit(solution)/shard_map/broadcast_in_dim | solution.py:508
Async XLA Ops:
  1.3 0.7 copy-start
  2.0 0.7 copy-start.1
where the time goes:
time: 72.6 us; the launch traced here: 72.4 us
  Pallas kernels  68.2 us (94%)
  other arithmetic  1.54 us (2%)
  local copies, waits for them, and re-layouts  1.33 us (2%)
  between operations  1.29 us (2%)
    pallas_call x1, Pallas kernels, fused(): pl.pallas_call(functools.partial(level, outer, width), out_shape=jax.Shap...  68.2 us

commit v1 on v0

--- a/solution.py
+++ b/solution.py
@@ -72,8 +72,10 @@
 MESH = pl.DeviceIdType.MESH
 WIRE = jnp.bfloat16
 STEP = 512
+CHUNK = 256
+EARLY = 0
 PART = 128
-LAG = 3
+LAG = 4
 NT = (((1,), (1,)), ((), ()))
 NN = (((1,), (0,)), ((), ()))
 
@@ -95,12 +97,12 @@
 
 
 def level(
-    outer, width,
-    x_ref, tail_ref, labels_ref, counts_ref, seeds_ref,
-    out_ref,
-    xf, table, gone, came, squares, cross, near, weights,
+    outer, width, scale,
+    x_ref, tail_ref, labels_hbm, counts_ref, seeds_hbm,
+    means_ref, occupancy_ref,
+    labels_ref, seeds_ref, xf, table, gone, came, squares, cross, near, weights,
     keep, csend, crecv, keepx, xsend, xrecv, zsend, zrecv,
-    x_load, y_out, y_in, u_out, d_out, t_out, t_in, c_out, c_in, x_out, x_in, z_out, z_in,
+    small_load, x_load, y_out, y_in, u_out, d_out, t_out, t_in, c_out, c_in, x_out, x_in, z_out, z_in,
 ):
     slots = xf.shape[2]
     shard = seeds_ref.shape[1]
@@ -128,16 +130,23 @@
         at = pl.ds(pl.multiple_of(c * STEP, STEP), STEP)
         return pltpu.make_async_copy(x_ref.at[at], xf.at[c], x_load.at[c])
 
-    @pl.loop(0, whole)
-    def _(c):
-        load(c).start()
-
     def remote(src, dst, out_sem, in_sem, where):
         return pltpu.make_async_remote_copy(
             src_ref=src, dst_ref=dst, send_sem=out_sem, recv_sem=in_sem,
             device_id=where, device_id_type=MESH,
         )
 
+    labels_load = pltpu.make_async_copy(labels_hbm, labels_ref, small_load.at[0])
+    seeds_load = pltpu.make_async_copy(seeds_hbm, seeds_ref, small_load.at[1])
+    labels_load.start()
+    seeds_load.start()
+
+    @pl.loop(0, whole)
+    def _(c):
+        load(c).start()
+
+    labels_load.wait()
+    seeds_load.wait()
     labels = labels_ref[...]
     spots = lax.broadcasted_iota(jnp.int32, (1, slots), 1)
     live = spots < counts_ref[0]
@@ -175,13 +184,21 @@
         act(y_copy(part, whole, last_rows))
 
     first = pick(0)
-    pl.semaphore_wait(barrier, outer + 2)
-
-    @pl.loop(0, whole)
-    def _(c):
+
+    def leave(c):
         at = pl.ds(pl.multiple_of(c * STEP, STEP), STEP)
         load(c).wait()
         gone[0, at, :] = dot(xf[c], first, NT).astype(jnp.bfloat16)
+
+    for c in range(EARLY):
+        leave(c)
+    pl.semaphore_wait(barrier, outer + 2)
+    for c in range(EARLY):
+        y_copy(0, c).start()
+
+    @pl.loop(EARLY, whole)
+    def _(c):
+        leave(c)
         y_copy(0, c).start()
 
     gone[0, pl.ds(whole * STEP, STEP), :] = dot(xf[whole], first, NT).astype(jnp.bfloat16)
@@ -349,16 +366,22 @@
             cross[...], norm, width, flag
         )
 
+    last = width % CHUNK
+    chunks = width // CHUNK + 1
+
+    def column(c):
+        return pl.multiple_of(lax.rem(c + chunks - 1, chunks) * CHUNK, CHUNK)
+
     def narrow(c, ref, sums):
         ref[...] = sums.astype(WIRE)
 
-        @pl.when(c == whole)
-        def _():
-            low = rest // PART * PART
+        @pl.when(c == 0)
+        def _():
+            low = last // PART * PART
             tile = sums[:, low : low + PART]
             lost = pltpu.roll(tile - tile.astype(WIRE).astype(jnp.float32), 1, 1)
             lane = lax.broadcasted_iota(jnp.int32, tile.shape, 1)
-            tile = jnp.where(lane == rest - low + 1, tile + lost, tile)
+            tile = jnp.where(lane == last - low + 1, tile + lost, tile)
             ref[:, low : low + PART] = tile.astype(WIRE)
 
     def c_copy(c):
@@ -374,9 +397,11 @@
         )
 
     def add_up(c):
-        at = pl.ds(pl.multiple_of(c * STEP, STEP), STEP)
+        place = column(c)
+        at = pl.ds(place, CHUNK)
+        within = pl.ds(pl.multiple_of(place % STEP, CHUNK), CHUNK)
         block = jnp.concatenate(
-            [xf[c]] + [came[part, at, :] for part in range(parts)], axis=1
+            [xf[place // STEP, within]] + [came[part, at, :] for part in range(parts)], axis=1
         )
         sums = dot(weights[...], block, NT)
         csend[c] = sums[half_k:]
@@ -399,13 +424,13 @@
             z_copy(c, d).start()
         keepx[c, pl.ds(0, shard), :] = sums[:shard]
 
-    @pl.loop(0, steps + LAG)
+    @pl.loop(0, chunks + LAG)
     def _(c):
-        @pl.when(c < steps)
+        @pl.when(c < chunks)
         def _():
             add_up(c)
 
-        @pl.when((c > 0) & (c <= steps))
+        @pl.when((c > 0) & (c <= chunks))
         def _():
             to_across(c - 1)
 
@@ -413,13 +438,22 @@
         def _():
             to_along(c - LAG)
 
-    @pl.loop(0, steps)
-    def _(c):
+    def total(c):
         sums = keepx[c, pl.ds(0, shard), :]
         for d in range(1, outer):
             z_copy(c, d).wait_recv()
             sums += zrecv[c, d - 1].astype(jnp.float32)
-        out_ref[:, pl.ds(pl.multiple_of(c * STEP, STEP), STEP)] = sums
+        return sums
+
+    sums = total(0)
+    mass = sums[:, last : last + 1] + sums[:, last + 1 : last + 2]
+    means_ref[:, pl.ds(width - last, last)] = sums[:, :last] / (mass + 1.0)
+    turned = jnp.sum(jnp.where(diagonal, mass, 0.0), axis=0, keepdims=True)
+    occupancy_ref[...] = turned * scale
+
+    @pl.loop(1, chunks)
+    def _(c):
+        means_ref[:, pl.ds(column(c), CHUNK)] = total(c) / (mass + 1.0)
 
     for copy in x_gather + c_gather:
         copy.wait_send()
@@ -435,7 +469,7 @@
     for part in range(parts):
         each_y(part, lambda copy: copy.wait_send())
 
-    @pl.loop(0, steps)
+    @pl.loop(0, chunks)
     def _(c):
         c_copy(c).wait_send()
         x_copy(c).wait_send()
@@ -456,22 +490,30 @@
     parts = slots // 2 // PART
     padded = round_up(width + 1, STEP)
     steps = padded // STEP
+    chunks = width // CHUNK + 1
+    total_slots = slots * lax.axis_size("half") * n_rows
+    scale = 2.0 * whole_k / total_slots
     dma = pltpu.SemaphoreType.DMA
     bf16, f32 = jnp.bfloat16, jnp.float32
     flops = 4 * (slots + slots // 2) * whole_k * width
     vmem = pl.BlockSpec(memory_space=pltpu.VMEM)
-    sums = pl.pallas_call(
-        functools.partial(level, outer, width),
-        out_shape=jax.ShapeDtypeStruct((shard, padded), f32),
+    hbm = pl.BlockSpec(memory_space=pltpu.HBM)
+    means, occupancy = pl.pallas_call(
+        functools.partial(level, outer, width, scale),
+        out_shape=(
+            jax.ShapeDtypeStruct((shard, width), f32),
+            jax.ShapeDtypeStruct((1, shard), f32),
+        ),
         grid=(1,),
         in_specs=[
-            pl.BlockSpec(memory_space=pltpu.HBM),
+            hbm,
             pl.BlockSpec((STEP, slots), lambda i: (steps - 1, 0)),
-            vmem, pl.BlockSpec(memory_space=pltpu.SMEM),
-            vmem,
+            hbm, pl.BlockSpec(memory_space=pltpu.SMEM), hbm,
         ],
-        out_specs=vmem,
+        out_specs=(vmem, vmem),
         scratch_shapes=[
+            pltpu.VMEM((1, slots), jnp.int32),
+            pltpu.VMEM((1, shard), jnp.int32),
             pltpu.VMEM((steps, STEP, slots), bf16),
             pltpu.VMEM((whole_k, padded), bf16),
             pltpu.VMEM((parts, padded, PART), bf16),
@@ -480,20 +522,20 @@
             pltpu.VMEM((whole_k, PART), f32),
             pltpu.VMEM((whole_k, slots), f32),
             pltpu.VMEM((whole_k, slots + parts * PART), bf16),
-            pltpu.VMEM((steps, whole_k // 2, STEP), f32),
-            pltpu.VMEM((steps, whole_k // 2, STEP), f32),
-            pltpu.VMEM((steps, whole_k // 2, STEP), f32),
-            pltpu.VMEM((steps, whole_k // 4, STEP), f32),
-            pltpu.VMEM((steps, whole_k // 4, STEP), WIRE),
-            pltpu.VMEM((steps, whole_k // 4, STEP), WIRE),
-            pltpu.VMEM((steps, outer - 1, shard, STEP), WIRE),
-            pltpu.VMEM((steps, outer - 1, shard, STEP), WIRE),
-            dma((steps,)), dma((parts, steps)), dma((parts, steps)),
+            pltpu.VMEM((chunks, whole_k // 2, CHUNK), f32),
+            pltpu.VMEM((chunks, whole_k // 2, CHUNK), f32),
+            pltpu.VMEM((chunks, whole_k // 2, CHUNK), f32),
+            pltpu.VMEM((chunks, whole_k // 4, CHUNK), f32),
+            pltpu.VMEM((chunks, whole_k // 4, CHUNK), WIRE),
+            pltpu.VMEM((chunks, whole_k // 4, CHUNK), WIRE),
+            pltpu.VMEM((chunks, outer - 1, shard, CHUNK), WIRE),
+            pltpu.VMEM((chunks, outer - 1, shard, CHUNK), WIRE),
+            dma((2,)), dma((steps,)), dma((parts, steps)), dma((parts, steps)),
             dma((outer,)), dma((outer,)),
             dma((4 * outer,)), dma((4 * outer,)),
-            dma((steps,)), dma((steps,)),
-            dma((steps,)), dma((steps,)),
-            dma((steps, outer - 1)), dma((steps, outer - 1)),
+            dma((chunks,)), dma((chunks,)),
+            dma((chunks,)), dma((chunks,)),
+            dma((chunks, outer - 1)), dma((chunks, outer - 1)),
         ],
         compiler_params=pltpu.CompilerParams(
             collective_id=0, has_side_effects=True, vmem_limit_bytes=52 * 2**20
@@ -501,11 +543,12 @@
         cost_estimate=pl.CostEstimate(
             flops=flops, bytes_accessed=slots * width * 2, transcendentals=slots * whole_k
         ),
-    )(frames.T, frames.T, labels[None], counts, seeds)
-    mass = sums[:, width] + sums[:, width + 1]
-    total_slots = slots * lax.axis_size("half") * n_rows
-    means = sums[:, :width] / (mass + 1.0)[:, None]
-    return (means[None], (mass * (2.0 * whole_k / total_slots))[None])
+    )(
+        frames.T, frames.T,
+        pltpu.with_memory_space_constraint(labels[None], pltpu.HBM), counts,
+        pltpu.with_memory_space_constraint(seeds, pltpu.HBM),
+    )
+    return (means[None], occupancy)
 
 
 def fits(mesh, frames, seeds):

time: 72.6 us -> 70.3 us (0.968)
  other arithmetic: 1.54 us -> 0 us
    broadcast_in_dim x1 -> x0, other arithmetic: 0.84 us -> none  [fused(): return (means[None], (mass * (2.0 * whole_k / total_slots))[None])]
where the time goes in v1:
time: 70.3 us; the launch traced here: 70.1 us
  Pallas kernels  67.6 us (96%)
  between operations  1.29 us (2%)
  local copies, waits for them, and re-layouts  1.26 us (2%)
    pallas_call x1, Pallas kernels, fused(): pl.pallas_call(functools.partial(level, outer, width, scale), out_shape=(...  67.6 us

profile of v1, /device:TPU:0, one launch (start us, length us, event | category | flops | bytes accessed | tf_op | source)
XLA Modules:
  0.0 70.1 jit_solution(10123286928742133428)
XLA Ops:
  1.3 67.6 %shard_map.59 = (f32[32,3000]{1,0:T(8,128)S(1)}, f32[1,32]{1,0:T(1,128)S(1)}) custom-call(bf16[3000,512]{1,0:T(8,128)(2,1)} %bitcast.4, bf16[3000,512]{1,0:T(8,128)(2,1)} %bitcast.5, s32[1,512]{1,0:T(1,128)} %bitcast.6, s32[1]{0:T(128)S(6)} %copy.8.counts_ref, s32[1,32]{1,0:T(1,128)} %seeds_hbm.1), custom_call_target="tpu_custom_call" | custom-call | flops 4718592000 | bytes 3072000 | tf_op jit(solution)/shard_map/pallas_call | solution.py:501
  68.9 0.7 %copy.9 = f32[1,32,3000]{2,1,0:T(8,128)} copy(f32[1,32,3000]{2,1,0:T(8,128)S(1)} %bitcast.3) | data formatting | bytes 768000
  69.6 0.5 copy.10

commit v2 on v1

--- a/solution.py
+++ b/solution.py
@@ -72,10 +72,14 @@
 MESH = pl.DeviceIdType.MESH
 WIRE = jnp.bfloat16
 STEP = 512
+TILE = 16
+EIGHT = 8
 CHUNK = 256
 EARLY = 0
 PART = 128
 LAG = 4
+TURN = 1
+BACK = 8
 NT = (((1,), (1,)), ((), ()))
 NN = (((1,), (0,)), ((), ()))
 
@@ -98,11 +102,12 @@
 
 def level(
     outer, width, scale,
-    x_ref, tail_ref, labels_hbm, counts_ref, seeds_hbm,
+    x_ref, odd_ref, labels_hbm, counts_ref, seeds_hbm,
     means_ref, occupancy_ref,
-    labels_ref, seeds_ref, xf, table, gone, came, squares, cross, near, weights,
+    labels_ref, seeds_ref, odd, xf, table, gone, came, squares, cross, near, weights,
     keep, csend, crecv, keepx, xsend, xrecv, zsend, zrecv,
-    small_load, x_load, y_out, y_in, u_out, d_out, t_out, t_in, c_out, c_in, x_out, x_in, z_out, z_in,
+    keept, zturn, zcame, xturn, xcame,
+    small_load, x_load, y_out, y_in, u_out, d_out, t_out, t_in, c_out, c_in, x_out, x_in, z_out, z_in, zt_out, zt_in, xt_out, xt_in,
 ):
     slots = xf.shape[2]
     shard = seeds_ref.shape[1]
@@ -121,47 +126,51 @@
         ((row // 4 + d) % outer) * 4 + row % 4 for d in range(1, outer)
     ]
 
+    even = rest // TILE * TILE
+
+    def load(c):
+        if isinstance(c, int) and c == whole:
+            at = pl.ds(whole * STEP, even)
+            return pltpu.make_async_copy(x_ref.at[at], xf.at[c, pl.ds(0, even)], x_load.at[c])
+        at = pl.ds(pl.multiple_of(c * STEP, STEP), STEP)
+        return pltpu.make_async_copy(x_ref.at[at], xf.at[c], x_load.at[c])
+
+    labels_load = pltpu.make_async_copy(labels_hbm, labels_ref, small_load.at[0])
+    seeds_load = pltpu.make_async_copy(seeds_hbm, seeds_ref, small_load.at[1])
+    odd_load = pltpu.make_async_copy(odd_ref.at[width // EIGHT - 1], odd, small_load.at[2])
+    labels_load.start()
+    load(0).start()
+
     barrier = pltpu.get_barrier_semaphore()
     pl.semaphore_signal(barrier, inc=1, device_id=(1 - side, row), device_id_type=MESH)
     for peer in [twin, across] + along:
         pl.semaphore_signal(barrier, inc=1, device_id=(side, peer), device_id_type=MESH)
 
-    def load(c):
-        at = pl.ds(pl.multiple_of(c * STEP, STEP), STEP)
-        return pltpu.make_async_copy(x_ref.at[at], xf.at[c], x_load.at[c])
-
     def remote(src, dst, out_sem, in_sem, where):
         return pltpu.make_async_remote_copy(
             src_ref=src, dst_ref=dst, send_sem=out_sem, recv_sem=in_sem,
             device_id=where, device_id_type=MESH,
         )
 
-    labels_load = pltpu.make_async_copy(labels_hbm, labels_ref, small_load.at[0])
-    seeds_load = pltpu.make_async_copy(seeds_hbm, seeds_ref, small_load.at[1])
-    labels_load.start()
-    seeds_load.start()
-
-    @pl.loop(0, whole)
+    @pl.loop(1, whole)
     def _(c):
         load(c).start()
 
-    labels_load.wait()
-    seeds_load.wait()
-    labels = labels_ref[...]
+    load(whole).start()
+    odd_load.start()
+    seeds_load.start()
     spots = lax.broadcasted_iota(jnp.int32, (1, slots), 1)
-    live = spots < counts_ref[0]
-    native = (live & (labels == side)).astype(jnp.float32)
-    foreign = jnp.where(live & (labels != side), 1.0, 0.0)
     upper = (
         lax.broadcasted_iota(jnp.int32, (slots, slots), 0)
         <= lax.broadcasted_iota(jnp.int32, (slots, slots), 1)
     ).astype(jnp.float32).astype(jnp.bfloat16)
+    live = spots < counts_ref[0]
+    labels_load.wait()
+    labels = labels_ref[...]
+    native = (live & (labels == side)).astype(jnp.float32)
+    foreign = jnp.where(live & (labels != side), 1.0, 0.0)
     rank = dot(jnp.broadcast_to(foreign, (16, slots)).astype(jnp.bfloat16), upper, NN)[:1]
     place = jnp.where(foreign > 0, rank - 1.0, -1.0).astype(jnp.int32)
-
-    xf[whole, pl.ds(0, rest), :] = tail_ref[pl.ds(0, rest), :]
-    fill = lax.broadcasted_iota(jnp.int32, (STEP - rest, slots), 0) == 0
-    xf[whole, pl.ds(rest, STEP - rest), :] = fill.astype(jnp.float32).astype(jnp.bfloat16)
 
     def pick(part):
         lane = lax.broadcasted_iota(jnp.int32, (PART, slots), 0) + part * PART
@@ -201,9 +210,18 @@
         leave(c)
         y_copy(0, c).start()
 
+    load(whole).wait()
+    odd_load.wait()
+    ones = lax.broadcasted_iota(jnp.int32, (STEP - even, slots), 0) == rest - even
+    fill = ones.astype(jnp.float32)
+    if rest > even:
+        fill = jnp.concatenate([odd[...].astype(jnp.float32), fill[rest - even :]], axis=0)
+    xf[whole, pl.ds(even, STEP - even), :] = fill.astype(jnp.bfloat16)
+
     gone[0, pl.ds(whole * STEP, STEP), :] = dot(xf[whole], first, NT).astype(jnp.bfloat16)
     y_copy(0, whole, last_rows).start()
 
+    seeds_load.wait()
     seeds = jnp.broadcast_to(seeds_ref[...], (shard, shard))
     diagonal = lax.broadcasted_iota(jnp.int32, (shard, shard), 0) == lax.broadcasted_iota(
         jnp.int32, (shard, shard), 1
@@ -408,6 +426,36 @@
         c_copy(c).start()
         keep[c] = sums[:half_k]
 
+    def zt_copy(d):
+        return remote(
+            zturn.at[d - 1], zcame.at[d - 1], zt_out.at[d - 1], zt_in.at[d - 1],
+            (side, along[d - 1]),
+        )
+
+    def xt_copy():
+        return remote(xturn, xcame, xt_out.at[0], xt_in.at[0], (side, across))
+
+    def turn_along(c):
+        c_copy(c).wait_recv()
+        sums = keep[c] + crecv[c]
+        for d in range(1, outer):
+            near_rows = sums[d * shard : (d + 1) * shard]
+            far_rows = sums[quarter_k + d * shard : quarter_k + (d + 1) * shard]
+            zturn[d - 1, pl.ds(0, shard), :] = near_rows.astype(WIRE)
+            zturn[d - 1, pl.ds(shard, shard), :] = far_rows.astype(WIRE)
+            zt_copy(d).start()
+        keept[pl.ds(0, shard), :] = sums[:shard]
+        keept[pl.ds(shard, shard), :] = sums[quarter_k : quarter_k + shard]
+
+    def turn_across():
+        sums = keept[...]
+        for d in range(1, outer):
+            zt_copy(d).wait_recv()
+            sums += zcame[d - 1].astype(jnp.float32)
+        xturn[...] = sums[shard:].astype(WIRE)
+        xt_copy().start()
+        keept[pl.ds(0, shard), :] = sums[:shard]
+
     def to_across(c):
         c_copy(c).wait_recv()
         sums = keep[c] + crecv[c]
@@ -430,13 +478,21 @@
         def _():
             add_up(c)
 
-        @pl.when((c > 0) & (c <= chunks))
+        @pl.when((c > 0) & (c <= chunks) & (c != TURN + 1))
         def _():
             to_across(c - 1)
 
-        @pl.when(c >= LAG)
+        @pl.when(c == TURN + 1)
+        def _():
+            turn_along(TURN)
+
+        @pl.when((c >= LAG) & (c != LAG + TURN))
         def _():
             to_along(c - LAG)
+
+        @pl.when(c == min(BACK, chunks + LAG - 1))
+        def _():
+            turn_across()
 
     def total(c):
         sums = keepx[c, pl.ds(0, shard), :]
@@ -451,7 +507,11 @@
     turned = jnp.sum(jnp.where(diagonal, mass, 0.0), axis=0, keepdims=True)
     occupancy_ref[...] = turned * scale
 
-    @pl.loop(1, chunks)
+    xt_copy().wait_recv()
+    sums = keept[pl.ds(0, shard), :] + xcame[...].astype(jnp.float32)
+    means_ref[:, pl.ds(column(TURN), CHUNK)] = sums / (mass + 1.0)
+
+    @pl.loop(TURN + 1, chunks)
     def _(c):
         means_ref[:, pl.ds(column(c), CHUNK)] = total(c) / (mass + 1.0)
 
@@ -472,9 +532,16 @@
     @pl.loop(0, chunks)
     def _(c):
         c_copy(c).wait_send()
-        x_copy(c).wait_send()
-        for d in range(1, outer):
-            z_copy(c, d).wait_send()
+
+        @pl.when(c != TURN)
+        def _():
+            x_copy(c).wait_send()
+            for d in range(1, outer):
+                z_copy(c, d).wait_send()
+
+    xt_copy().wait_send()
+    for d in range(1, outer):
+        zt_copy(d).wait_send()
 
 
 def y_rows(width):
@@ -504,16 +571,15 @@
             jax.ShapeDtypeStruct((shard, width), f32),
             jax.ShapeDtypeStruct((1, shard), f32),
         ),
-        grid=(1,),
         in_specs=[
             hbm,
-            pl.BlockSpec((STEP, slots), lambda i: (steps - 1, 0)),
-            hbm, pl.BlockSpec(memory_space=pltpu.SMEM), hbm,
+            hbm, hbm, pl.BlockSpec(memory_space=pltpu.SMEM), hbm,
         ],
         out_specs=(vmem, vmem),
         scratch_shapes=[
             pltpu.VMEM((1, slots), jnp.int32),
             pltpu.VMEM((1, shard), jnp.int32),
+            pltpu.VMEM((EIGHT, slots), bf16),
             pltpu.VMEM((steps, STEP, slots), bf16),
             pltpu.VMEM((whole_k, padded), bf16),
             pltpu.VMEM((parts, padded, PART), bf16),
@@ -530,12 +596,18 @@
             pltpu.VMEM((chunks, whole_k // 4, CHUNK), WIRE),
             pltpu.VMEM((chunks, outer - 1, shard, CHUNK), WIRE),
             pltpu.VMEM((chunks, outer - 1, shard, CHUNK), WIRE),
-            dma((2,)), dma((steps,)), dma((parts, steps)), dma((parts, steps)),
+            pltpu.VMEM((2 * shard, CHUNK), f32),
+            pltpu.VMEM((outer - 1, 2 * shard, CHUNK), WIRE),
+            pltpu.VMEM((outer - 1, 2 * shard, CHUNK), WIRE),
+            pltpu.VMEM((shard, CHUNK), WIRE),
+            pltpu.VMEM((shard, CHUNK), WIRE),
+            dma((3,)), dma((steps,)), dma((parts, steps)), dma((parts, steps)),
             dma((outer,)), dma((outer,)),
             dma((4 * outer,)), dma((4 * outer,)),
             dma((chunks,)), dma((chunks,)),
             dma((chunks,)), dma((chunks,)),
             dma((chunks, outer - 1)), dma((chunks, outer - 1)),
+            dma((outer - 1,)), dma((outer - 1,)), dma((1,)), dma((1,)),
         ],
         compiler_params=pltpu.CompilerParams(
             collective_id=0, has_side_effects=True, vmem_limit_bytes=52 * 2**20
@@ -544,7 +616,7 @@
             flops=flops, bytes_accessed=slots * width * 2, transcendentals=slots * whole_k
         ),
     )(
-        frames.T, frames.T,
+        frames.T, frames.T.reshape(width // EIGHT, EIGHT, slots),
         pltpu.with_memory_space_constraint(labels[None], pltpu.HBM), counts,
         pltpu.with_memory_space_constraint(seeds, pltpu.HBM),
     )
@@ -556,7 +628,7 @@
     n_half, n_rows = sizes["half"], sizes["rows"]
     slots = frames.shape[0] // (n_half * n_rows)
     shard = seeds.shape[1] // n_rows
-    lone = frames.shape[1] % STEP > 0 and frames.shape[1] % PART < PART - 1
+    lone = frames.shape[1] % EIGHT == 0 and frames.shape[1] % STEP > 0 and frames.shape[1] % PART < PART - 1
     return (
         n_half == 2 and n_rows % 4 == 0 and n_rows >= 8 and shard % 16 == 0 and shard > 0
         and slots % (2 * PART) == 0 and slots * n_half * n_rows == frames.shape[0]

time: 70.3 us -> 68.4 us (0.973)
  Pallas kernels: 67.6 us -> 65.7 us
    pallas_call x1, Pallas kernels: 67.6 us -> 65.7 us  [fused(): pl.pallas_call(functools.partial(level, outer, width, scale), out_shape=(...]
where the time goes in v2:
time: 68.4 us; the launch traced here: 68.3 us
  Pallas kernels  65.7 us (96%)
  between operations  1.29 us (2%)
  local copies, waits for them, and re-layouts  1.26 us (2%)
    pallas_call x1, Pallas kernels, fused(): pl.pallas_call(functools.partial(level, outer, width, scale), out_shape=(...  65.7 us

profile of v2, /device:TPU:0, one launch (start us, length us, event | category | flops | bytes accessed | tf_op | source)
XLA Modules:
  0.0 68.3 jit_solution(13645523157830115810)
XLA Ops:
  1.3 65.7 %shard_map.59 = (f32[32,3000]{1,0:T(8,128)S(1)}, f32[1,32]{1,0:T(1,128)S(1)}) custom-call(bf16[3000,512]{1,0:T(8,128)(2,1)} %bitcast.6, bf16[375,8,512]{2,1,0:T(8,128)(2,1)} %bitcast.7, s32[1,512]{1,0:T(1,128)} %bitcast.8, s32[1]{0:T(128)S(6)} %copy.8.counts_ref, s32[1,32]{1,0:T(1,128)} %seeds_hbm.1), custom_call_target="tpu_custom_call" | custom-call | flops 4718592000 | bytes 3072000 | tf_op jit(solution)/shard_map/pallas_call | solution.py:568
  67.0 0.7 %copy.9 = f32[1,32,3000]{2,1,0:T(8,128)} copy(f32[1,32,3000]{2,1,0:T(8,128)S(1)} %bitcast.5) | data formatting | bytes 768000
  67.7 0.5 copy.10

commit v3 on v2

--- a/solution.py
+++ b/solution.py
@@ -75,7 +75,8 @@
 TILE = 16
 EIGHT = 8
 CHUNK = 256
-EARLY = 0
+EARLY = 1
+AHEAD = 3
 PART = 128
 LAG = 4
 TURN = 1
@@ -138,13 +139,13 @@
     labels_load = pltpu.make_async_copy(labels_hbm, labels_ref, small_load.at[0])
     seeds_load = pltpu.make_async_copy(seeds_hbm, seeds_ref, small_load.at[1])
     odd_load = pltpu.make_async_copy(odd_ref.at[width // EIGHT - 1], odd, small_load.at[2])
-    labels_load.start()
-    load(0).start()
-
     barrier = pltpu.get_barrier_semaphore()
     pl.semaphore_signal(barrier, inc=1, device_id=(1 - side, row), device_id_type=MESH)
     for peer in [twin, across] + along:
         pl.semaphore_signal(barrier, inc=1, device_id=(side, peer), device_id_type=MESH)
+
+    labels_load.start()
+    load(0).start()
 
     def remote(src, dst, out_sem, in_sem, where):
         return pltpu.make_async_remote_copy(
@@ -362,7 +363,35 @@
     norm = jnp.sum(squares[...], axis=1, keepdims=True)
     weights[:, pl.ds(0, slots)] = column_weights(near[...], norm, width, native)
 
+    last = width % CHUNK
+    chunks = width // CHUNK + 1
+
+    def column(c):
+        return pl.multiple_of(lax.rem(c + chunks - 1, chunks) * CHUNK, CHUNK)
+
+    def weigh(c, parts_in, native_in):
+        place = column(c)
+        at = pl.ds(place, CHUNK)
+        within = pl.ds(pl.multiple_of(place % STEP, CHUNK), CHUNK)
+        block = [xf[place // STEP, within]] if native_in else []
+        block += [came[part, at, :] for part in parts_in]
+        first_lane = 0 if native_in else slots + parts_in[0] * PART
+        count = (slots if native_in else 0) + len(parts_in) * PART
+        return dot(
+            weights[:, pl.ds(first_lane, count)],
+            block[0] if len(block) == 1 else jnp.concatenate(block, axis=1), NT,
+        )
+
+    def begin_sums():
+        @pl.loop(0, AHEAD)
+        def _(c):
+            sums = weigh(c, list(range(parts - 1)), True)
+            csend[c] = sums[half_k:]
+            keep[c] = sums[:half_k]
+
     for part in range(parts):
+        if part == parts - 1:
+            begin_sums()
         cross[...] = jnp.zeros_like(cross)
 
         @pl.loop(0, steps)
@@ -383,12 +412,6 @@
         weights[:, pl.ds(slots + part * PART, PART)] = column_weights(
             cross[...], norm, width, flag
         )
-
-    last = width % CHUNK
-    chunks = width // CHUNK + 1
-
-    def column(c):
-        return pl.multiple_of(lax.rem(c + chunks - 1, chunks) * CHUNK, CHUNK)
 
     def narrow(c, ref, sums):
         ref[...] = sums.astype(WIRE)
@@ -415,16 +438,19 @@
         )
 
     def add_up(c):
-        place = column(c)
-        at = pl.ds(place, CHUNK)
-        within = pl.ds(pl.multiple_of(place % STEP, CHUNK), CHUNK)
-        block = jnp.concatenate(
-            [xf[place // STEP, within]] + [came[part, at, :] for part in range(parts)], axis=1
-        )
-        sums = dot(weights[...], block, NT)
-        csend[c] = sums[half_k:]
-        c_copy(c).start()
-        keep[c] = sums[:half_k]
+        @pl.when(c < AHEAD)
+        def _():
+            sums = weigh(c, [parts - 1], False)
+            csend[c] += sums[half_k:]
+            c_copy(c).start()
+            keep[c] += sums[:half_k]
+
+        @pl.when(c >= AHEAD)
+        def _():
+            sums = weigh(c, list(range(parts)), True)
+            csend[c] = sums[half_k:]
+            c_copy(c).start()
+            keep[c] = sums[:half_k]
 
     def zt_copy(d):
         return remote(
@@ -472,7 +498,7 @@
             z_copy(c, d).start()
         keepx[c, pl.ds(0, shard), :] = sums[:shard]
 
-    @pl.loop(0, chunks + LAG)
+    @pl.loop(0, chunks + 1)
     def _(c):
         @pl.when(c < chunks)
         def _():
@@ -490,7 +516,7 @@
         def _():
             to_along(c - LAG)
 
-        @pl.when(c == min(BACK, chunks + LAG - 1))
+        @pl.when(c == BACK)
         def _():
             turn_across()
 
@@ -501,20 +527,32 @@
             sums += zrecv[c, d - 1].astype(jnp.float32)
         return sums
 
+    def finish(c):
+        means_ref[:, pl.ds(column(c), CHUNK)] = total(c) / (mass + 1.0)
+        sent_chunk(c)
+
+    def sent_chunk(c):
+        c_copy(c).wait_send()
+        x_copy(c).wait_send()
+        for d in range(1, outer):
+            z_copy(c, d).wait_send()
+
     sums = total(0)
     mass = sums[:, last : last + 1] + sums[:, last + 1 : last + 2]
     means_ref[:, pl.ds(width - last, last)] = sums[:, :last] / (mass + 1.0)
     turned = jnp.sum(jnp.where(diagonal, mass, 0.0), axis=0, keepdims=True)
     occupancy_ref[...] = turned * scale
+    sent_chunk(0)
+    pl.loop(TURN + 1, TURN + 3)(finish)
+    to_along(chunks - 3)
 
     xt_copy().wait_recv()
     sums = keept[pl.ds(0, shard), :] + xcame[...].astype(jnp.float32)
     means_ref[:, pl.ds(column(TURN), CHUNK)] = sums / (mass + 1.0)
-
-    @pl.loop(TURN + 1, chunks)
-    def _(c):
-        means_ref[:, pl.ds(column(c), CHUNK)] = total(c) / (mass + 1.0)
-
+    c_copy(TURN).wait_send()
+    xt_copy().wait_send()
+    for d in range(1, outer):
+        zt_copy(d).wait_send()
     for copy in x_gather + c_gather:
         copy.wait_send()
     for k in range(outer - 1):
@@ -526,22 +564,12 @@
         def _():
             up_copy(k).wait_send()
 
+    to_along(chunks - 2)
     for part in range(parts):
         each_y(part, lambda copy: copy.wait_send())
-
-    @pl.loop(0, chunks)
-    def _(c):
-        c_copy(c).wait_send()
-
-        @pl.when(c != TURN)
-        def _():
-            x_copy(c).wait_send()
-            for d in range(1, outer):
-                z_copy(c, d).wait_send()
-
-    xt_copy().wait_send()
-    for d in range(1, outer):
-        zt_copy(d).wait_send()
+    pl.loop(TURN + 3, TURN + 5)(finish)
+    to_along(chunks - 1)
+    pl.loop(TURN + 5, chunks)(finish)
 
 
 def y_rows(width):
@@ -633,7 +661,7 @@
         n_half == 2 and n_rows % 4 == 0 and n_rows >= 8 and shard % 16 == 0 and shard > 0
         and slots % (2 * PART) == 0 and slots * n_half * n_rows == frames.shape[0]
         and slots <= 1024 and seeds.shape[1] <= 512 and frames.shape[1] <= 4096
-        and frames.shape[1] > STEP and lone
+        and frames.shape[1] // CHUNK >= max(BACK, TURN + 6) and lone
     )
 
 

time: 68.4 us -> 67.9 us (level)
  no operation moved by 1% of the time
where the time goes in v3:
time: 67.9 us; the launch traced here: 67.7 us
  Pallas kernels  65.2 us (96%)
  between operations  1.29 us (2%)
  local copies, waits for them, and re-layouts  1.26 us (2%)
    pallas_call x1, Pallas kernels, fused(): pl.pallas_call(functools.partial(level, outer, width, scale), out_shape=(...  65.2 us

profile of v3, /device:TPU:0, one launch (start us, length us, event | category | flops | bytes accessed | tf_op | source)
XLA Modules:
  0.0 67.7 jit_solution(16164238751633072324)
XLA Ops:
  1.3 65.2 %shard_map.59 = (f32[32,3000]{1,0:T(8,128)S(1)}, f32[1,32]{1,0:T(1,128)S(1)}) custom-call(bf16[3000,512]{1,0:T(8,128)(2,1)} %bitcast.6, bf16[375,8,512]{2,1,0:T(8,128)(2,1)} %bitcast.7, s32[1,512]{1,0:T(1,128)} %bitcast.8, s32[1]{0:T(128)S(6)} %copy.8.counts_ref, s32[1,32]{1,0:T(1,128)} %seeds_hbm.1), custom_call_target="tpu_custom_call" | custom-call | flops 4718592000 | bytes 3072000 | tf_op jit(solution)/shard_map/pallas_call | solution.py:596
  66.5 0.7 %copy.9 = f32[1,32,3000]{2,1,0:T(8,128)} copy(f32[1,32,3000]{2,1,0:T(8,128)S(1)} %bitcast.5) | data formatting | bytes 768000
  67.2 0.5 copy.10

commit v4 on v3

--- a/solution.py
+++ b/solution.py
@@ -516,10 +516,6 @@
         def _():
             to_along(c - LAG)
 
-        @pl.when(c == BACK)
-        def _():
-            turn_across()
-
     def total(c):
         sums = keepx[c, pl.ds(0, shard), :]
         for d in range(1, outer):
@@ -545,7 +541,23 @@
     sent_chunk(0)
     pl.loop(TURN + 1, TURN + 3)(finish)
     to_along(chunks - 3)
-
+    turn_across()
+    to_along(chunks - 2)
+    pl.loop(TURN + 3, TURN + 5)(finish)
+    to_along(chunks - 1)
+    for copy in x_gather + c_gather:
+        copy.wait_send()
+    for k in range(outer - 1):
+        @pl.when((depth > 0) & (depth + k <= outer - 1))
+        def _():
+            down_copy(k).wait_send()
+
+        @pl.when((depth < outer - 1) & (depth >= k))
+        def _():
+            up_copy(k).wait_send()
+
+    for part in range(parts):
+        each_y(part, lambda copy: copy.wait_send())
     xt_copy().wait_recv()
     sums = keept[pl.ds(0, shard), :] + xcame[...].astype(jnp.float32)
     means_ref[:, pl.ds(column(TURN), CHUNK)] = sums / (mass + 1.0)
@@ -553,22 +565,6 @@
     xt_copy().wait_send()
     for d in range(1, outer):
         zt_copy(d).wait_send()
-    for copy in x_gather + c_gather:
-        copy.wait_send()
-    for k in range(outer - 1):
-        @pl.when((depth > 0) & (depth + k <= outer - 1))
-        def _():
-            down_copy(k).wait_send()
-
-        @pl.when((depth < outer - 1) & (depth >= k))
-        def _():
-            up_copy(k).wait_send()
-
-    to_along(chunks - 2)
-    for part in range(parts):
-        each_y(part, lambda copy: copy.wait_send())
-    pl.loop(TURN + 3, TURN + 5)(finish)
-    to_along(chunks - 1)
     pl.loop(TURN + 5, chunks)(finish)
 
 

time: 67.9 us -> 67.7 us (level)
  no operation moved by 1% of the time
where the time goes in v4:
time: 67.7 us; the launch traced here: 67.6 us
  Pallas kernels  65 us (96%)
  between operations  1.29 us (2%)
  local copies, waits for them, and re-layouts  1.26 us (2%)
    pallas_call x1, Pallas kernels, fused(): pl.pallas_call(functools.partial(level, outer, width, scale), out_shape=(...  65 us

profile of v4, /device:TPU:0, one launch (start us, length us, event | category | flops | bytes accessed | tf_op | source)
XLA Modules:
  0.0 67.6 jit_solution(14162266949577368625)
XLA Ops:
  1.3 65.0 %shard_map.59 = (f32[32,3000]{1,0:T(8,128)S(1)}, f32[1,32]{1,0:T(1,128)S(1)}) custom-call(bf16[3000,512]{1,0:T(8,128)(2,1)} %bitcast.6, bf16[375,8,512]{2,1,0:T(8,128)(2,1)} %bitcast.7, s32[1,512]{1,0:T(1,128)} %bitcast.8, s32[1]{0:T(128)S(6)} %copy.8.counts_ref, s32[1,32]{1,0:T(1,128)} %seeds_hbm.1), custom_call_target="tpu_custom_call" | custom-call | flops 4718592000 | bytes 3072000 | tf_op jit(solution)/shard_map/pallas_call | solution.py:592
  66.3 0.7 %copy.9 = f32[1,32,3000]{2,1,0:T(8,128)} copy(f32[1,32,3000]{2,1,0:T(8,128)S(1)} %bitcast.5) | data formatting | bytes 768000
  67.1 0.5 copy.10

commit v5 on v4

--- a/solution.py
+++ b/solution.py
@@ -498,7 +498,9 @@
             z_copy(c, d).start()
         keepx[c, pl.ds(0, shard), :] = sums[:shard]
 
-    @pl.loop(0, chunks + 1)
+    add_up(0)
+
+    @pl.loop(1, chunks + 1)
     def _(c):
         @pl.when(c < chunks)
         def _():

time: 67.7 us -> 67.7 us (level)
  no operation moved by 1% of the time
where the time goes in v5:
time: 67.7 us; the launch traced here: 67.5 us
  Pallas kernels  64.9 us (96%)
  between operations  1.29 us (2%)
  local copies, waits for them, and re-layouts  1.26 us (2%)
    pallas_call x1, Pallas kernels, fused(): pl.pallas_call(functools.partial(level, outer, width, scale), out_shape=(...  64.9 us

profile of v5, /device:TPU:0, one launch (start us, length us, event | category | flops | bytes accessed | tf_op | source)
XLA Modules:
  0.0 67.5 jit_solution(12130726275691821673)
XLA Ops:
  1.3 64.9 %shard_map.59 = (f32[32,3000]{1,0:T(8,128)S(1)}, f32[1,32]{1,0:T(1,128)S(1)}) custom-call(bf16[3000,512]{1,0:T(8,128)(2,1)} %bitcast.6, bf16[375,8,512]{2,1,0:T(8,128)(2,1)} %bitcast.7, s32[1,512]{1,0:T(1,128)} %bitcast.8, s32[1]{0:T(128)S(6)} %copy.8.counts_ref, s32[1,32]{1,0:T(1,128)} %seeds_hbm.1), custom_call_target="tpu_custom_call" | custom-call | flops 4718592000 | bytes 3072000 | tf_op jit(solution)/shard_map/pallas_call | solution.py:594
  66.2 0.7 %copy.9 = f32[1,32,3000]{2,1,0:T(8,128)} copy(f32[1,32,3000]{2,1,0:T(8,128)S(1)} %bitcast.5) | data formatting | bytes 768000
  67.0 0.5 copy.10
